TPU v7x, 32 devices: a whole 2x2x4 slice. The times are simulated.
32 devices in a mesh: groups: 2 (over y), tile: 4 (over z), segment: 2 (over core), mp: 2 (over x).
Axes of the slice: x: 2, y: 2, z: 4, core: 2. Of those that a mesh axis runs over, the one named last changes fastest.
Arguments:
- spectra: bfloat16 [2, 64, 48, 224], P(None, ('groups', 'tile')), parts along dimension 1, may hold values from -6 to 6
- valid: int32 [2, 64], P(None, 'groups'), parts along dimension 1, may hold values from 1 to 48, as said below
- project: bfloat16 [224, 16], replicated, may hold values from -0.375 to 0.375
- enc_in: bfloat16 [768, 3072], P(None, 'mp'), may hold values from -0.21875 to 0.21875
- enc_out: bfloat16 [3072, 768], P('mp'), may hold values from -0.109375 to 0.109375
- tok_embed: bfloat16 [48, 2048], replicated, may hold values from -0.875 to 0.875
- band_embed: bfloat16 [16, 2048], P('tile'), may hold values from -3 to 3
- dec_in: bfloat16 [2048, 8192], P('tile', 'mp'), may hold values from -0.125 to 0.125
- dec_out: bfloat16 [8192, 2048], P('mp', 'tile'), may hold values from -0.0625 to 0.0625
- head: bfloat16 [2048, 672], P('tile', 'mp'), may hold values from -0.125 to 0.125
Outputs:
- grad_project: float32 [448, 16], P(('groups', 'tile', 'segment')), parts along dimension 0
- grad_enc_in: float32 [1536, 3072], P(('groups', 'tile', 'segment'), 'mp'), parts along dimension 0
- grad_enc_out: float32 [6144, 768], P(('groups', 'mp'), ('tile', 'segment')), parts along dimension 0
There are 2 independent parts, one for each index of `groups`. A program takes and returns all parts, laid end to end along the dimension named above; an argument that names none is the same for every part. Nothing has to cross between parts.
Inputs may be any that keep to these rules, and one draw needn't show every extreme that they name: Pixels of patch n in micro-batch m with index below valid[m, n] count in the loss.
All inputs are finite; a program needn't handle non-finite values.
Results may differ from a plain program's by a relative error of at most 0.018.
Values may be sent and summed in bfloat16 or wider, within the bound.
A program may use at most 128 MiB of HBM per device.

v0:
```python
import jax
import jax.numpy as jnp
from jax import lax
from jax.sharding import PartitionSpec as P

BF = jnp.bfloat16
F32 = jnp.float32


def inv_rms(values):
    return lax.rsqrt(jnp.mean(values * values, axis=-1, keepdims=True) + 1e-05)


def rms_back(values, gradient):
    scaling = inv_rms(values)
    normed = values * scaling
    return scaling * (gradient - normed * jnp.mean(gradient * normed, axis=-1, keepdims=True))


def gelu(v):
    return 0.5 * v * (1 + jnp.tanh(0.7978845608028654 * (v + 0.044715 * v * v * v)))


def gelu_and_slope(v):
    square = v * v
    t = jnp.tanh(0.7978845608028654 * v * (1 + 0.044715 * square))
    half = 0.5 * (1 + t)
    slope = half + 0.5 * v * (1 - t * t) * 0.7978845608028654 * (1 + 3 * 0.044715 * square)
    return (v * half, slope)


def dot(a, b):
    return jnp.dot(a, b, preferred_element_type=F32)


def dot_t(a, b):
    return lax.dot_general(a, b, (((1,), (1,)), ((), ())), preferred_element_type=F32)


def t_dot(a, b):
    return lax.dot_general(a, b, (((0,), (0,)), ((), ())), preferred_element_type=F32)


def body(spectra, valid, project, enc_in, enc_out, tok_embed, band_embed, dec_in, dec_out, head):
    tile, seg, mp = (lax.axis_index(a) for a in ("tile", "segment", "mp"))
    T, S, M = (lax.axis_size(a) for a in ("tile", "segment", "mp"))
    batches, per_tile, pixels, bands = spectra.shape
    codes = project.shape[1]
    width = bands // codes
    local = batches * per_tile
    share = local // (S * M)
    rows = T * local
    student = codes * pixels
    dim = tok_embed.shape[1]
    dt = dec_in.shape[0]
    hid = dec_in.shape[1] // S
    once = jnp.logical_and(seg == 0, mp == 0).astype(F32)
    patches = spectra.reshape(local, pixels, bands)
    flat = patches.reshape(local * pixels, bands)
    feat_local = (
        dot(flat, project)
        .astype(BF)
        .reshape(local, pixels, codes)
        .transpose(0, 2, 1)
        .reshape(local, student)
    )
    feats = lax.all_gather(feat_local, "tile")
    feats = feats.reshape(T, S, M, share, student).transpose(1, 2, 0, 3, 4).reshape(rows, student)
    band_all = lax.all_gather(band_embed, "tile", tiled=True)
    head_full = lax.all_gather(head, "mp", axis=1, tiled=True)
    embed = jnp.concatenate([tok_embed, band_all], axis=0)
    embed_z = lax.dynamic_slice_in_dim(embed, tile * dt, dt, 1)
    d_in = lax.dynamic_slice_in_dim(dec_in, seg * hid, hid, 1)
    d_out = lax.dynamic_slice_in_dim(dec_out, seg * hid, hid, 0)
    folded = lax.psum(dot(embed_z, d_in).astype(BF), "tile")
    fold_tok, fold_band = (folded[:pixels], folded[pixels:])
    feats32 = feats.astype(F32)
    normed = (feats32 * inv_rms(feats32)).astype(BF)
    pre_act, pre_slope = gelu_and_slope(dot(normed, enc_in))
    act_out = pre_act.astype(BF)
    summed = lax.psum(dot(act_out, enc_out).astype(BF), "mp").astype(F32)
    encoded = (feats32 + summed).astype(BF)
    tokens = rows * codes
    tok = encoded.reshape(tokens, pixels)
    embedded = (
        (dot(tok, tok_embed).reshape(rows, codes, dim) + band_all.astype(F32))
        .reshape(tokens, dim)
        .astype(BF)
    )
    scaling = inv_rms(embedded.astype(F32))
    hid_pre = scaling * (
        dot(tok, fold_tok).reshape(rows, codes, hid) + fold_band.astype(F32)
    ).reshape(tokens, hid)
    hid_act, hid_slope = gelu_and_slope(hid_pre)
    embedded_z = lax.dynamic_slice_in_dim(embedded, tile * dt, dt, 1)
    decoded = (once * embedded_z.astype(F32) + dot(hid_act.astype(BF), d_out)).astype(BF)
    partial = dot(decoded, head_full).astype(BF)
    own = lax.psum_scatter(
        partial.reshape(S * M, T, share * codes, -1), ("segment", "mp"), scatter_dimension=0
    )
    own = lax.psum_scatter(own, "tile", scatter_dimension=0).astype(F32)
    quarter = (seg * M + mp) * share
    own_patches = lax.dynamic_slice_in_dim(patches, quarter, share, 0)
    target = (
        own_patches.reshape(share, pixels, codes, width)
        .transpose(0, 2, 1, 3)
        .reshape(share * codes, -1)
    )
    total_valid = jnp.sum(valid.astype(F32))
    loss_scale = 2.0 * batches * valid.shape[1] / total_valid
    own_valid = lax.dynamic_slice_in_dim(valid, tile * per_tile, per_tile, 1).reshape(local)
    own_valid = lax.dynamic_slice_in_dim(own_valid, quarter, share, 0)
    column = jnp.arange(pixels * width, dtype=jnp.int32) // width
    mask = (column[None, :] < jnp.repeat(own_valid, codes)[:, None]).astype(F32)
    grad_own = (loss_scale * mask * (own - target.astype(F32))).astype(BF)
    grad_rebuilt = lax.all_gather(lax.all_gather(grad_own, "tile"), ("segment", "mp")).reshape(
        tokens, -1
    )
    grad_decoded = dot_t(grad_rebuilt, head_full).astype(BF)
    grad_hid = hid_slope * dot_t(grad_decoded, d_out)
    tok_z = lax.dynamic_slice_in_dim(tok_embed, tile * dt, dt, 1)
    unit_tok = dot_t((embedded.astype(F32) * scaling).astype(BF), tok_embed)
    along = jnp.sum(grad_hid * hid_pre, axis=1, keepdims=True) / dim
    grad_tok = scaling * (dot_t(grad_hid.astype(BF), fold_tok) - unit_tok * along)
    grad_tok = grad_tok + once * dot_t(grad_decoded, tok_z)
    grad_encoded = lax.psum(grad_tok.reshape(rows, student).astype(BF), ("tile", "segment", "mp"))
    grad_act = (pre_slope * dot_t(grad_encoded, enc_out)).astype(BF)
    columns = student // (T * S)
    start = (tile * S + seg) * columns
    grad_out = t_dot(act_out, lax.dynamic_slice_in_dim(grad_encoded, start, columns, 1))
    grad_in = t_dot(lax.dynamic_slice_in_dim(normed, start, columns, 1), grad_act)
    grad_normed = lax.psum(dot_t(grad_act, enc_in).astype(BF), "mp").astype(F32)
    own_rows = lambda a: lax.dynamic_slice_in_dim(
        a.reshape(S * M, T, share, student), tile, 1, 1
    ).reshape(local, student)
    grad_feat = (
        own_rows(grad_encoded).astype(F32) + rms_back(feat_local.astype(F32), own_rows(grad_normed))
    ).astype(BF)
    grad_codes = grad_feat.reshape(local, codes, pixels).transpose(0, 2, 1).reshape(-1, codes)
    grad_proj = jnp.sum(lax.all_gather(t_dot(flat, grad_codes), "tile"), axis=0)
    proj_rows = bands // (T * S)
    grad_proj = lax.dynamic_slice_in_dim(grad_proj, (tile * S + seg) * proj_rows, proj_rows, 0)
    return (grad_proj, grad_in, grad_out)


def solution(mesh):
    placed = (
        P(None, ("groups", "tile"), None, None),
        P(None, "groups"),
        P(),
        P(None, "mp"),
        P("mp", None),
        P(),
        P("tile", None),
        P("tile", "mp"),
        P("mp", "tile"),
        P("tile", "mp"),
    )
    return jax.shard_map(
        body,
        mesh=mesh,
        in_specs=placed,
        out_specs=(
            P(("groups", "tile", "segment"), None),
            P(("groups", "tile", "segment"), "mp"),
            P(("groups", "mp"), ("tile", "segment")),
        ),
        check_vma=False,
    )
```

profile of v0, /device:TPU:0, one launch (start us, length us, event | category | flops | bytes accessed | tf_op | source)
XLA Modules:
  0.0 350.5 jit_solution(10092934858017082224)
XLA Ops:
  7.2 1.4 convolution_convert_fusion.5
  8.6 0.2 reshape.254
  8.8 0.7 fusion.49
  9.4 0.1 all_gather_reshape.3
  9.6 15.0 %all_gather.25 = bf16[4,16,768]{2,1,0:T(8,128)(2,1)S(1)} all-gather(bf16[1,16,768]{2,1,0:T(8,128)(2,1)S(1)} %all_gather_reshape.3), channel_id=1, replica_groups=mesh['groups'=2,'tile'=4,'segment'=2,'mp'=2] {'tile'}, dimensions={0}, use_global_device_ids=true | all-gather | bytes 122880 | tf_op jit(solution)/shard_map/all_gather | solution.py:67
  24.7 0.1 multiply_reduce_fusion.2
  25.0 0.1 rsqrt.35
  25.1 0.1 multiply_convert_fusion.7
  25.2 2.2 fusion.50
  27.4 0.7 copy-done.3
  28.2 1.2 convolution_convert_fusion.4
  29.5 13.3 %all-gather.2 = bf16[4,4,2048]{2,1,0:T(4,128)(2,1)S(1)} all-gather(bf16[1,4,2048]{2,1,0:T(4,128)(2,1)S(1)} %bitcast.88), channel_id=1, replica_groups=mesh['groups'=2,'tile'=4,'segment'=2,'mp'=2] {'tile'}, dimensions={0}, use_global_device_ids=true | all-gather | bytes 81920 | tf_op jit(solution)/shard_map/all_gather | solution.py:69
  42.8 2.8 convolution_convert_fusion
  45.7 0.7 convert_element_type.165
  46.4 8.4 %all_gather.27 = bf16[512,672]{0,1:T(8,128)(2,1)S(1)} all-gather(bf16[512,336]{0,1:T(8,128)(2,1)} %param.19), channel_id=1, replica_groups=mesh['groups'=2,'tile'=4,'segment'=2,'mp'=2] {'mp'}, dimensions={1}, use_global_device_ids=true | all-gather | bytes 1032192 | tf_op jit(solution)/shard_map/all_gather | solution.py:70
  54.7 1.0 add_convert_fusion.2
  55.8 0.3 dot_general.61
  56.1 4.2 %multiply_reduce_fusion.1 = (f32[64,16]{1,0:T(8,128)S(1)}, bf16[64,16,2048]{2,1,0:T(8,128)(2,1)}) fusion(f32[16,2048]{1,0:T(8,128)} %convert_element_type.165, bf16[64,16,48]{2,1,0:T(8,128)(2,1)S(1)} %dot_general.61, bf16[48,2048]{1,0:T(8,128)(2,1)} %param.15), kind=kOutput, calls=%fused_computation.7 | convolution fusion | flops 211811328 | bytes 4624384 | tf_op jit(solution)/shard_map/dot_general | solution.py:33
  60.4 29.6 %all-reduce.7.cloned.1.call-done = bf16[64,2048]{1,0:T(8,128)(2,1)} async-done(((bf16[64,2048]{1,0:T(8,128)(2,1)}), bf16[64,2048]{1,0:T(8,128)(2,1)}) %all-reduce.7.cloned.1.call-update) | async-done | bytes 262160 | tf_op jit(solution)/shard_map/psum | solution.py:75
  90.0 0.8 slice_convert_fusion
  90.8 2.2 convolution_add_fusion
  93.0 5.3 %multiply_convert_fusion.1 = bf16[1024,2048]{1,0:T(8,128)(2,1)} fusion(f32[64,16,2048]{2,1,0:T(8,128)S(1)} %convolution_add_fusion, f32[1024]{0:T(1024)S(1)} %rsqrt.37), kind=kLoop, calls=%fused_computation.3 | loop fusion | flops 20971520 | bytes 12587008 | tf_op jit(solution)/shard_map/convert_element_type | solution.py:96
  98.3 7.2 %convolution_convert_fusion.1 = bf16[1024,672]{0,1:T(8,128)(2,1)} fusion(bf16[512,672]{0,1:T(8,128)(2,1)S(1)} %all_gather.27, bf16[1024,2048]{1,0:T(8,128)(2,1)} %multiply_convert_fusion.1, bf16[4096,512]{1,0:T(8,128)(2,1)} %param.18, s32[]{:T(128)S(6)} %select_n.37, bf16[1024,2048]{1,0:T(8,128)(2,1)} %bitcast.90, s32[]{:T(128)S(6)} %select_n.36, ...), kind=kOutput, calls=%fused_computation.22 | convolution fusion | flops 2854912000 | bytes 9404428 | tf_op jit(solution)/shard_map/dot_general | solution.py:33
  105.5 2.6 copy.40
  108.2 28.0 %reduce-scatter.3.cloned.1.call-done = bf16[1,4,64,672]{3,2,1,0:T(8,128)(2,1)} async-done(((bf16[4,4,64,672]{3,2,1,0:T(8,128)(2,1)}), bf16[1,4,64,672]{3,2,1,0:T(8,128)(2,1)}) %reduce-scatter.3.cloned.1.call-update) | async-done | bytes 344080 | tf_op jit(solution)/shard_map/reduce_scatter | solution.py:98
  136.6 0.1 lt.54
  136.7 0.2 copy.49
  136.9 1.8 copy.42
  138.7 1.9 reshape.268
  140.7 0.6 convert_reduce_fusion
  142.0 17.0 %reduce-scatter.5.cloned.1.call-done = bf16[1,64,672]{2,1,0:T(8,128)(2,1)} async-done(((bf16[4,64,672]{2,1,0:T(8,128)(2,1)}), bf16[1,64,672]{2,1,0:T(8,128)(2,1)}) %reduce-scatter.5.cloned.1.call-update) | async-done | bytes 86032 | tf_op jit(solution)/shard_map/reduce_scatter | solution.py:101
  159.0 1.0 multiply_convert_fusion.6
  160.0 15.8 %all_gather.28 = bf16[4,64,672]{2,1,0:T(8,128)(2,1)} all-gather(bf16[1,64,672]{2,1,0:T(8,128)(2,1)S(1)} %multiply_convert_fusion.6), channel_id=1, replica_groups=mesh['groups'=2,'tile'=4,'segment'=2,'mp'=2] {'tile'}, dimensions={0}, use_global_device_ids=true | all-gather | bytes 430080 | tf_op jit(solution)/shard_map/all_gather | solution.py:116
  175.8 0.2 all-reduce.9.cloned.1.call-start
  176.0 0.2 multiply_reduce_fusion.3
  176.2 17.2 %all-gather.6.cloned.1.call-done = bf16[16,64,672]{2,1,0:T(8,128)(2,1)} async-done(((bf16[4,64,672]{2,1,0:T(8,128)(2,1)}), bf16[16,64,672]{2,1,0:T(8,128)(2,1)}) %all-gather.6.cloned.1.call-update) | async-done | bytes 1376272 | tf_op jit(solution)/shard_map/all_gather | solution.py:116
  193.4 2.7 convolution_convert_fusion.2
  196.1 0.2 copy-done.12
  196.3 9.2 %multiply_reduce_fusion = (f32[1024]{0:T(1024)S(1)}, bf16[1024,2048]{1,0:T(8,128)(2,1)S(1)}) fusion(f32[64,16,2048]{2,1,0:T(8,128)} %copy-done.1, f32[1024]{0:T(1024)S(1)} %rsqrt.37, bf16[1024,512]{1,0:T(8,128)(2,1)S(1)} %convolution_convert_fusion.2, bf16[4096,512]{1,0:T(8,128)(2,1)S(1)} %copy-done.12, s32[]{:T(128)S(6)} %select_n.37), kind=kOutput, calls=%fused_computation.1 | convolution fusion | flops 2191522816 | bytes 15736836 | tf_op jit(solution)/shard_map/dot_general | solution.py:37
  205.5 0.4 convolution_multiply_fusion.1
  206.0 1.5 fusion.20
  207.5 2.0 fusion.21
  209.5 1.1 copy.43
  210.6 0.9 convert_element_type.188
  211.6 1.0 reshape.270
  212.7 86.1 %all-reduce.9.cloned.1.call-done = bf16[64,768]{1,0:T(8,128)(2,1)} async-done(((bf16[64,768]{1,0:T(8,128)(2,1)}), bf16[64,768]{1,0:T(8,128)(2,1)}) %all-reduce.9.cloned.1.call-update) | async-done | bytes 98320 | tf_op jit(solution)/shard_map/psum | solution.py:126
  298.8 1.7 fusion.4
  300.5 3.1 convolution_convert_fusion.3
  303.7 1.9 fusion.36
  305.6 0.9 reshape.261
  306.5 0.7 copy.45
  307.2 1.9 fusion.34
  309.1 0.9 reshape.260
  310.1 0.1 reshape.269
  310.2 17.2 %all-reduce.11.cloned.1.call-done = bf16[4,4,4,768]{3,2,0,1:T(4,128)(2,1)} async-done(((bf16[4,4,4,768]{3,2,0,1:T(4,128)(2,1)}), bf16[4,4,4,768]{3,2,0,1:T(4,128)(2,1)}) %all-reduce.11.cloned.1.call-update) | async-done | bytes 98320 | tf_op jit(solution)/shard_map/psum | solution.py:132
  327.4 0.9 multiply_reduce_fusion.4
  328.3 0.1 div.44
  328.4 0.7 dynamic-slice_convert_fusion.1
  329.1 0.1 reshape.263
  329.2 0.1 fusion.30
  329.4 0.1 reshape.264
  329.5 0.1 convolution_bitcast_fusion
  329.7 13.3 %all-gather.3 = f32[4,224,16]{1,2,0:T(8,128)S(1)} all-gather(f32[1,224,16]{1,2,0:T(8,128)S(1)} %convolution_bitcast_fusion), channel_id=3, replica_groups=mesh['groups'=2,'tile'=4,'segment'=2,'mp'=2] {'tile'}, dimensions={0}, use_global_device_ids=true | all-gather | bytes 71680 | tf_op jit(solution)/shard_map/all_gather | solution.py:140
  342.9 0.7 constant_dynamic-slice_fusion
  (62 shorter events, 1.3 us)
Async XLA Ops:
  7.2 21.0 %copy-start = (bf16[1536,768]{1,0:T(8,128)(2,1)S(1)}, bf16[1536,768]{1,0:T(8,128)(2,1)}, u32[]{:S(2)}) copy-start(bf16[1536,768]{1,0:T(8,128)(2,1)} %param.14) | copy-start | bytes 7077892
  7.2 22.3 %copy-start.10 = (bf16[4,2048]{1,0:T(4,128)(2,1)S(1)}, bf16[4,2048]{1,0:T(4,128)(2,1)}, u32[]{:S(2)}) copy-start(bf16[4,2048]{1,0:T(4,128)(2,1)} %param.16) | copy-start | bytes 49156
  7.2 47.6 %all-reduce.5.cloned.1.call-start = ((), (), s32[]{:S(2)}) async-start(), calls=%async_computation.2 | async-start | bytes 196608 | tf_op jit(solution)/shard_map/psum | solution.py:81
  7.2 35.6 %copy-start.8 = (bf16[48,2048]{1,0:T(8,128)(2,1)S(1)}, bf16[48,2048]{1,0:T(8,128)(2,1)}, u32[]{:S(2)}) copy-start(bf16[48,2048]{1,0:T(8,128)(2,1)} %param.15) | copy-start | bytes 589828
  25.2 4.3 %copy-start.7 = (bf16[64,768]{1,0:T(8,128)(2,1)}, bf16[64,768]{1,0:T(8,128)(2,1)S(1)}, u32[]{:S(2)}) copy-start(bf16[64,768]{1,0:T(8,128)(2,1)S(1)} %multiply_convert_fusion.7) | copy-start | bytes 294916
  27.4 0.8 copy-start.3
  29.4 60.6 %all-reduce.7.cloned.1.call-start = ((), (), s32[]{:S(2)}) async-start(), calls=%async_computation.3 | async-start | bytes 524288 | tf_op jit(solution)/shard_map/psum | solution.py:75
  45.6 90.6 %reduce-scatter.3.cloned.1.call-start = ((), (), s32[]{:S(2)}) async-start(), calls=%async_computation.4 | async-start | bytes 1966080 | tf_op jit(solution)/shard_map/reduce_scatter | solution.py:98
  54.7 43.5 %copy-start.6 = (bf16[512,672]{0,1:T(8,128)(2,1)}, bf16[512,672]{0,1:T(8,128)(2,1)S(1)}, u32[]{:S(2)}) copy-start(bf16[512,672]{0,1:T(8,128)(2,1)S(1)} %all_gather.27) | copy-start | bytes 2064388
  93.0 5.3 %copy-start.1 = (f32[64,16,2048]{2,1,0:T(8,128)}, f32[64,16,2048]{2,1,0:T(8,128)S(1)}, u32[]{:S(2)}) copy-start(f32[64,16,2048]{2,1,0:T(8,128)S(1)} %convolution_add_fusion) | copy-start | bytes 25165828
  105.5 30.8 %copy-start.11 = (s32[2,32]{1,0:T(2,128)S(1)}, s32[2,32]{1,0:T(2,128)}, u32[]{:S(2)}) copy-start(s32[2,32]{1,0:T(2,128)} %param.11) | copy-start | bytes 772
  105.5 31.2 %copy-start.2 = (bf16[2,8,48,224]{3,2,1,0:T(8,128)(2,1)S(1)}, bf16[2,8,48,224]{3,2,1,0:T(8,128)(2,1)}, u32[]{:S(2)}) copy-start(bf16[2,8,48,224]{3,2,1,0:T(8,128)(2,1)} %param.10) | copy-start | bytes 1032196
  108.1 50.8 %reduce-scatter.5.cloned.1.call-start = ((), (), s32[]{:S(2)}) async-start(), calls=%async_computation.5 | async-start | bytes 491520 | tf_op jit(solution)/shard_map/reduce_scatter | solution.py:101
  136.2 57.2 %all-gather.6.cloned.1.call-start = ((), (), s32[]{:S(2)}) async-start(), calls=%async_computation.8 | async-start | bytes 1966080 | tf_op jit(solution)/shard_map/all_gather | solution.py:116
  175.8 123.0 %all-reduce.9.cloned.1.call-start = ((), (), s32[]{:S(2)}) async-start(), calls=%async_computation.6 | async-start | bytes 196608 | tf_op jit(solution)/shard_map/psum | solution.py:126
  193.4 2.9 copy-start.12
  196.3 9.2 %copy-start.9 = (bf16[48,2048]{1,0:T(8,128)(2,1)S(1)}, bf16[48,2048]{1,0:T(8,128)(2,1)}, u32[]{:S(2)}) copy-start(bf16[48,2048]{1,0:T(8,128)(2,1)} %param.15) | copy-start | bytes 589828
  196.3 9.7 %copy-start.13 = (bf16[64,16,2048]{2,1,0:T(8,128)(2,1)S(1)}, bf16[64,16,2048]{2,1,0:T(8,128)(2,1)}, u32[]{:S(2)}) copy-start(bf16[64,16,2048]{2,1,0:T(8,128)(2,1)} %get-tuple-element.6) | copy-start | bytes 12582916
  206.0 1.5 copy-start.5
  207.5 91.4 %copy-start.4 = (f32[64,1536]{1,0:T(8,128)S(1)}, f32[64,1536]{1,0:T(8,128)}, u32[]{:S(2)}) copy-start(f32[64,1536]{1,0:T(8,128)} %copy-done.3) | copy-start | bytes 1179652
  211.5 115.9 %all-reduce.11.cloned.1.call-start = ((), (), s32[]{:S(2)}) async-start(), calls=%async_computation.7 | async-start | bytes 196608 | tf_op jit(solution)/shard_map/psum | solution.py:132
Sparse Core Ops, SparseCore 0:
  29.5 22.1 all-reduce.4
  54.6 35.3 all-reduce.6
  108.3 27.9 reduce-scatter.2
  138.3 20.5 reduce-scatter.4
  175.9 17.4 all-gather.5
  211.6 87.1 all-reduce.8
  307.3 20.0 all-reduce.10
where the time goes:
time: 351 us; the launch traced here: 350 us
  waiting for transfers between devices  195 us (56%)
  blocking collectives  65.8 us (19%)
  matrix products  45.8 us (13%)
  local copies, waits for them, and re-layouts  15.7 us (4%)
  between operations  15.2 us (4%)
  other arithmetic  12.3 us (4%)
    psum x1, waiting for transfers between devices, body(): lax.psum(grad_tok.reshape(rows, student).astype(BF), ('tile', 'segment',...  86.1 us
    psum x1, waiting for transfers between devices, body(): folded = lax.psum(dot(embed_z, d_in).astype(BF), 'tile')  29.6 us
    reduce_scatter x1, waiting for transfers between devices, body(): lax.psum_scatter(partial.reshape(S * M, T, share * codes, -1), ('segment'...  28 us
    dot_general x7, matrix products, dot(): return jnp.dot(a, b, preferred_element_type=F32)  21.1 us
    dot_general x7, matrix products, dot_t(): lax.dot_general(a, b, (((1,), (1,)), ((), ())), preferred_element_type=F32)  20.7 us
    all_gather x1, waiting for transfers between devices, body(): lax.all_gather(lax.all_gather(grad_own, 'tile'), ('segment', 'mp'))  17.2 us
    psum x1, waiting for transfers between devices, body(): grad_normed = lax.psum(dot_t(grad_act, enc_in).astype(BF), 'mp').astype(F32)  17.2 us
    reduce_scatter x1, waiting for transfers between devices, body(): own = lax.psum_scatter(own, 'tile', scatter_dimension=0).astype(F32)  17 us
  transfers between devices with their start and end apart: 7, of which 6 were waited for; matrix products, arithmetic and copies ran while one was open for 5% of the time, Pallas kernels for 0%

commit v1 on v0

--- a/solution.py
+++ b/solution.py
@@ -5,6 +5,11 @@
 
 BF = jnp.bfloat16
 F32 = jnp.float32
+
+
+def add_all(x, axis):
+    shards = lax.all_gather(x, axis)
+    return jnp.sum(shards, axis=0)
 
 
 def inv_rms(values):
@@ -123,7 +128,7 @@
     along = jnp.sum(grad_hid * hid_pre, axis=1, keepdims=True) / dim
     grad_tok = scaling * (dot_t(grad_hid.astype(BF), fold_tok) - unit_tok * along)
     grad_tok = grad_tok + once * dot_t(grad_decoded, tok_z)
-    grad_encoded = lax.psum(grad_tok.reshape(rows, student).astype(BF), ("tile", "segment", "mp"))
+    grad_encoded = add_all(grad_tok.reshape(rows, student).astype(BF), ("tile", "segment", "mp"))
     grad_act = (pre_slope * dot_t(grad_encoded, enc_out)).astype(BF)
     columns = student // (T * S)
     start = (tile * S + seg) * columns

time: 351 us -> 306 us (0.87)
  waiting for transfers between devices: 195 us -> 151 us
    psum x1 -> x0, waiting for transfers between devices: 86.1 us -> none  [body(): lax.psum(grad_tok.reshape(rows, student).astype(BF), ('tile', 'segment',...]
    all_gather x0 -> x1, waiting for transfers between devices: none -> 38.5 us  [add_all(): shards = lax.all_gather(x, axis)]
where the time goes in v1:
time: 306 us
  waiting for transfers between devices  151 us (49%)
  blocking collectives  65.8 us (22%)
  matrix products  43.6 us (14%)
  between operations  15.2 us (5%)
  local copies, waits for them, and re-layouts  14.8 us (5%)
  other arithmetic  14.6 us (5%)
    all_gather x1, waiting for transfers between devices, add_all(): shards = lax.all_gather(x, axis)  38.5 us
    psum x1, waiting for transfers between devices, body(): folded = lax.psum(dot(embed_z, d_in).astype(BF), 'tile')  29.6 us
    reduce_scatter x1, waiting for transfers between devices, body(): lax.psum_scatter(partial.reshape(S * M, T, share * codes, -1), ('segment'...  28 us
    dot_general x7, matrix products, dot(): return jnp.dot(a, b, preferred_element_type=F32)  21.1 us
    psum x1, waiting for transfers between devices, body(): grad_normed = lax.psum(dot_t(grad_act, enc_in).astype(BF), 'mp').astype(F32)  19.9 us
    dot_general x7, matrix products, dot_t(): lax.dot_general(a, b, (((1,), (1,)), ((), ())), preferred_element_type=F32)  18.5 us
    all_gather x1, waiting for transfers between devices, body(): lax.all_gather(lax.all_gather(grad_own, 'tile'), ('segment', 'mp'))  17.9 us
    reduce_scatter x1, waiting for transfers between devices, body(): own = lax.psum_scatter(own, 'tile', scatter_dimension=0).astype(F32)  17 us
  transfers between devices with their start and end apart: 7, of which 6 were waited for; matrix products, arithmetic and copies ran while one was open for 5% of the time, Pallas kernels for 0%

profile of v1, /device:TPU:0, one launch (start us, length us, event | category | flops | bytes accessed | tf_op | source)
XLA Modules:
  0.0 305.6 jit_solution(12642412171121853214)
XLA Ops:
  7.2 1.4 convolution_convert_fusion.5
  8.6 0.2 reshape.264
  8.8 0.7 fusion.49
  9.5 0.1 all_gather_reshape.3
  9.6 15.0 %all_gather.29 = bf16[4,16,768]{2,1,0:T(8,128)(2,1)S(1)} all-gather(bf16[1,16,768]{2,1,0:T(8,128)(2,1)S(1)} %all_gather_reshape.3), channel_id=1, replica_groups=mesh['groups'=2,'tile'=4,'segment'=2,'mp'=2] {'tile'}, dimensions={0}, use_global_device_ids=true | all-gather | bytes 122880 | tf_op jit(solution)/shard_map/all_gather | solution.py:72
  24.7 0.1 multiply_reduce_fusion.2
  25.0 0.1 rsqrt.35
  25.2 2.2 fusion.50
  27.5 0.7 copy-done.4
  28.2 1.2 convolution_convert_fusion.4
  29.5 13.3 %all-gather.2 = bf16[4,4,2048]{2,1,0:T(4,128)(2,1)S(1)} all-gather(bf16[1,4,2048]{2,1,0:T(4,128)(2,1)S(1)} %bitcast.84), channel_id=1, replica_groups=mesh['groups'=2,'tile'=4,'segment'=2,'mp'=2] {'tile'}, dimensions={0}, use_global_device_ids=true | all-gather | bytes 81920 | tf_op jit(solution)/shard_map/all_gather | solution.py:74
  42.8 2.8 convolution_convert_fusion
  45.7 0.7 convert_element_type.174
  46.3 8.4 %all_gather.31 = bf16[512,672]{0,1:T(8,128)(2,1)S(1)} all-gather(bf16[512,336]{0,1:T(8,128)(2,1)} %param.19), channel_id=1, replica_groups=mesh['groups'=2,'tile'=4,'segment'=2,'mp'=2] {'mp'}, dimensions={1}, use_global_device_ids=true | all-gather | bytes 1032192 | tf_op jit(solution)/shard_map/all_gather | solution.py:75
  54.7 1.0 add_convert_fusion.2
  55.7 0.3 dot_general.61
  56.0 4.2 %multiply_reduce_fusion.1 = (f32[64,16]{1,0:T(8,128)S(1)}, bf16[64,16,2048]{2,1,0:T(8,128)(2,1)}) fusion(f32[16,2048]{1,0:T(8,128)} %convert_element_type.174, bf16[64,16,48]{2,1,0:T(8,128)(2,1)S(1)} %dot_general.61, bf16[48,2048]{1,0:T(8,128)(2,1)} %param.15), kind=kOutput, calls=%fused_computation.7 | convolution fusion | flops 211811328 | bytes 4624384 | tf_op jit(solution)/shard_map/dot_general | solution.py:38
  60.4 29.6 %all-reduce.6.cloned.1.call-done = bf16[64,2048]{1,0:T(8,128)(2,1)} async-done(((bf16[64,2048]{1,0:T(8,128)(2,1)}), bf16[64,2048]{1,0:T(8,128)(2,1)}) %all-reduce.6.cloned.1.call-update) | async-done | bytes 262160 | tf_op jit(solution)/shard_map/psum | solution.py:80
  90.0 0.8 slice_convert_fusion
  90.8 2.2 convolution_add_fusion
  93.0 5.3 %multiply_convert_fusion.1 = bf16[1024,2048]{1,0:T(8,128)(2,1)} fusion(f32[64,16,2048]{2,1,0:T(8,128)S(1)} %convolution_add_fusion, f32[1024]{0:T(1024)S(1)} %rsqrt.37), kind=kLoop, calls=%fused_computation.3 | loop fusion | flops 20971520 | bytes 12587008 | tf_op jit(solution)/shard_map/convert_element_type | solution.py:101
  98.3 7.2 %convolution_convert_fusion.1 = bf16[1024,672]{0,1:T(8,128)(2,1)} fusion(bf16[512,672]{0,1:T(8,128)(2,1)S(1)} %all_gather.31, bf16[1024,2048]{1,0:T(8,128)(2,1)} %multiply_convert_fusion.1, bf16[4096,512]{1,0:T(8,128)(2,1)} %param.18, s32[]{:T(128)S(6)} %select_n.37, bf16[1024,2048]{1,0:T(8,128)(2,1)} %bitcast.86, s32[]{:T(128)S(6)} %select_n.36, ...), kind=kOutput, calls=%fused_computation.22 | convolution fusion | flops 2854912000 | bytes 9404428 | tf_op jit(solution)/shard_map/dot_general | solution.py:38
  105.5 2.6 copy.38
  108.2 28.0 %reduce-scatter.3.cloned.1.call-done = bf16[1,4,64,672]{3,2,1,0:T(8,128)(2,1)} async-done(((bf16[4,4,64,672]{3,2,1,0:T(8,128)(2,1)}), bf16[1,4,64,672]{3,2,1,0:T(8,128)(2,1)}) %reduce-scatter.3.cloned.1.call-update) | async-done | bytes 344080 | tf_op jit(solution)/shard_map/reduce_scatter | solution.py:103
  136.6 0.1 lt.54
  136.8 0.2 copy.45
  137.0 1.8 copy.40
  138.8 1.9 reshape.278
  140.7 0.6 convert_reduce_fusion
  142.0 17.0 %reduce-scatter.5.cloned.1.call-done = bf16[1,64,672]{2,1,0:T(8,128)(2,1)} async-done(((bf16[4,64,672]{2,1,0:T(8,128)(2,1)}), bf16[1,64,672]{2,1,0:T(8,128)(2,1)}) %reduce-scatter.5.cloned.1.call-update) | async-done | bytes 86032 | tf_op jit(solution)/shard_map/reduce_scatter | solution.py:106
  159.0 1.0 multiply_convert_fusion.6
  160.0 15.8 %all_gather.32 = bf16[4,64,672]{2,1,0:T(8,128)(2,1)} all-gather(bf16[1,64,672]{2,1,0:T(8,128)(2,1)S(1)} %multiply_convert_fusion.6), channel_id=1, replica_groups=mesh['groups'=2,'tile'=4,'segment'=2,'mp'=2] {'tile'}, dimensions={0}, use_global_device_ids=true | all-gather | bytes 430080 | tf_op jit(solution)/shard_map/all_gather | solution.py:121
  175.8 0.2 all-gather.7.cloned.1.call-start
  176.1 17.9 %all-gather.9.cloned.1.call-done = bf16[16,64,672]{2,1,0:T(8,128)(2,1)} async-done(((bf16[4,64,672]{2,1,0:T(8,128)(2,1)}), bf16[16,64,672]{2,1,0:T(8,128)(2,1)}) %all-gather.9.cloned.1.call-update) | async-done | bytes 1376272 | tf_op jit(solution)/shard_map/all_gather | solution.py:121
  194.0 2.7 convolution_convert_fusion.2
  196.7 0.2 copy-done.13
  196.8 9.2 %multiply_reduce_fusion = (f32[1024]{0:T(1024)S(1)}, bf16[1024,2048]{1,0:T(8,128)(2,1)S(1)}) fusion(f32[64,16,2048]{2,1,0:T(8,128)} %copy-done.1, f32[1024]{0:T(1024)S(1)} %rsqrt.37, bf16[1024,512]{1,0:T(8,128)(2,1)S(1)} %convolution_convert_fusion.2, bf16[4096,512]{1,0:T(8,128)(2,1)S(1)} %copy-done.13, s32[]{:T(128)S(6)} %select_n.37), kind=kOutput, calls=%fused_computation.1 | convolution fusion | flops 2191522816 | bytes 15736836 | tf_op jit(solution)/shard_map/dot_general | solution.py:42
  206.1 0.4 convolution_multiply_fusion.1
  206.5 1.5 fusion.20
  208.0 2.0 fusion.21
  210.0 1.1 copy.41
  211.1 0.9 convert_element_type.197
  212.1 1.0 reshape.280
  213.1 0.2 multiply_reduce_fusion.3
  213.3 0.1 rsqrt.39
  213.4 38.5 %all-gather.7.cloned.1.call-done = bf16[16,64,768]{2,1,0:T(8,128)(2,1)} async-done(((bf16[1,64,768]{2,1,0:T(8,128)(2,1)}), bf16[16,64,768]{2,1,0:T(8,128)(2,1)}) %all-gather.7.cloned.1.call-update) | async-done | bytes 1572880 | tf_op jit(solution)/shard_map/all_gather | solution.py:11
  251.9 2.3 reduce_sum.82
  254.2 1.9 fusion.4
  256.1 1.9 fusion.34
  258.0 1.9 fusion.36
  259.9 0.8 convolution_convert_fusion.3
  260.7 0.9 reshape.270
  261.7 0.7 copy.42
  262.4 0.1 reshape.279
  262.5 19.9 %all-reduce.8.cloned.1.call-done = bf16[4,4,4,768]{3,2,0,1:T(4,128)(2,1)} async-done(((bf16[4,4,4,768]{3,2,0,1:T(4,128)(2,1)}), bf16[4,4,4,768]{3,2,0,1:T(4,128)(2,1)}) %all-reduce.8.cloned.1.call-update) | async-done | bytes 98320 | tf_op jit(solution)/shard_map/psum | solution.py:137
  282.5 0.9 multiply_reduce_fusion.4
  283.4 0.1 div.44
  283.5 0.7 dynamic-slice_convert_fusion.1
  284.2 0.1 reshape.273
  284.4 0.1 fusion.30
  284.5 0.1 reshape.274
  284.6 0.1 convolution_bitcast_fusion
  284.8 13.3 %all-gather.3 = f32[4,224,16]{1,2,0:T(8,128)S(1)} all-gather(f32[1,224,16]{1,2,0:T(8,128)S(1)} %convolution_bitcast_fusion), channel_id=3, replica_groups=mesh['groups'=2,'tile'=4,'segment'=2,'mp'=2] {'tile'}, dimensions={0}, use_global_device_ids=true | all-gather | bytes 71680 | tf_op jit(solution)/shard_map/all_gather | solution.py:145
  298.0 0.7 constant_dynamic-slice_fusion
  (65 shorter events, 1.3 us)
Async XLA Ops:
  7.2 21.0 %copy-start = (bf16[1536,768]{1,0:T(8,128)(2,1)S(1)}, bf16[1536,768]{1,0:T(8,128)(2,1)}, u32[]{:S(2)}) copy-start(bf16[1536,768]{1,0:T(8,128)(2,1)} %param.14) | copy-start | bytes 7077892
  7.2 22.3 %copy-start.11 = (bf16[4,2048]{1,0:T(4,128)(2,1)S(1)}, bf16[4,2048]{1,0:T(4,128)(2,1)}, u32[]{:S(2)}) copy-start(bf16[4,2048]{1,0:T(4,128)(2,1)} %param.16) | copy-start | bytes 49156
  7.2 47.5 %all-reduce.4.cloned.1.call-start = ((), (), s32[]{:S(2)}) async-start(), calls=%async_computation.2 | async-start | bytes 196608 | tf_op jit(solution)/shard_map/psum | solution.py:86
  7.2 35.6 %copy-start.9 = (bf16[48,2048]{1,0:T(8,128)(2,1)S(1)}, bf16[48,2048]{1,0:T(8,128)(2,1)}, u32[]{:S(2)}) copy-start(bf16[48,2048]{1,0:T(8,128)(2,1)} %param.15) | copy-start | bytes 589828
  25.2 4.3 %copy-start.8 = (bf16[64,768]{1,0:T(8,128)(2,1)}, bf16[64,768]{1,0:T(8,128)(2,1)S(1)}, u32[]{:S(2)}) copy-start(bf16[64,768]{1,0:T(8,128)(2,1)S(1)} %multiply_convert_fusion.7) | copy-start | bytes 294916
  27.4 0.8 copy-start.4
  29.4 60.6 %all-reduce.6.cloned.1.call-start = ((), (), s32[]{:S(2)}) async-start(), calls=%async_computation.3 | async-start | bytes 524288 | tf_op jit(solution)/shard_map/psum | solution.py:80
  45.6 90.6 %reduce-scatter.3.cloned.1.call-start = ((), (), s32[]{:S(2)}) async-start(), calls=%async_computation.4 | async-start | bytes 1966080 | tf_op jit(solution)/shard_map/reduce_scatter | solution.py:103
  54.7 43.6 %copy-start.7 = (bf16[512,672]{0,1:T(8,128)(2,1)}, bf16[512,672]{0,1:T(8,128)(2,1)S(1)}, u32[]{:S(2)}) copy-start(bf16[512,672]{0,1:T(8,128)(2,1)S(1)} %all_gather.31) | copy-start | bytes 2064388
  93.0 5.3 %copy-start.1 = (f32[64,16,2048]{2,1,0:T(8,128)}, f32[64,16,2048]{2,1,0:T(8,128)S(1)}, u32[]{:S(2)}) copy-start(f32[64,16,2048]{2,1,0:T(8,128)S(1)} %convolution_add_fusion) | copy-start | bytes 25165828
  105.5 30.8 %copy-start.12 = (s32[2,32]{1,0:T(2,128)S(1)}, s32[2,32]{1,0:T(2,128)}, u32[]{:S(2)}) copy-start(s32[2,32]{1,0:T(2,128)} %param.11) | copy-start | bytes 772
  105.5 31.2 %copy-start.3 = (bf16[2,8,48,224]{3,2,1,0:T(8,128)(2,1)S(1)}, bf16[2,8,48,224]{3,2,1,0:T(8,128)(2,1)}, u32[]{:S(2)}) copy-start(bf16[2,8,48,224]{3,2,1,0:T(8,128)(2,1)} %param.10) | copy-start | bytes 1032196
  108.2 50.8 %reduce-scatter.5.cloned.1.call-start = ((), (), s32[]{:S(2)}) async-start(), calls=%async_computation.5 | async-start | bytes 491520 | tf_op jit(solution)/shard_map/reduce_scatter | solution.py:106
  136.3 57.7 %all-gather.9.cloned.1.call-start = ((), (), s32[]{:S(2)}) async-start(), calls=%async_computation.8 | async-start | bytes 1966080 | tf_op jit(solution)/shard_map/all_gather | solution.py:121
  175.8 76.1 %all-gather.7.cloned.1.call-start = ((), (), s32[]{:S(2)}) async-start(), calls=%async_computation.6 | async-start | bytes 1671168 | tf_op jit(solution)/shard_map/all_gather | solution.py:11
  194.0 2.9 copy-start.13
  196.8 9.2 %copy-start.10 = (bf16[48,2048]{1,0:T(8,128)(2,1)S(1)}, bf16[48,2048]{1,0:T(8,128)(2,1)}, u32[]{:S(2)}) copy-start(bf16[48,2048]{1,0:T(8,128)(2,1)} %param.15) | copy-start | bytes 589828
  196.8 9.7 %copy-start.14 = (bf16[64,16,2048]{2,1,0:T(8,128)(2,1)S(1)}, bf16[64,16,2048]{2,1,0:T(8,128)(2,1)}, u32[]{:S(2)}) copy-start(bf16[64,16,2048]{2,1,0:T(8,128)(2,1)} %get-tuple-element.6) | copy-start | bytes 12582916
  206.5 1.5 copy-start.6
  208.0 46.2 %copy-start.5 = (f32[64,1536]{1,0:T(8,128)S(1)}, f32[64,1536]{1,0:T(8,128)}, u32[]{:S(2)}) copy-start(f32[64,1536]{1,0:T(8,128)} %copy-done.4) | copy-start | bytes 1179652
  212.0 70.5 %all-reduce.8.cloned.1.call-start = ((), (), s32[]{:S(2)}) async-start(), calls=%async_computation.7 | async-start | bytes 196608 | tf_op jit(solution)/shard_map/psum | solution.py:137
  254.2 5.7 %copy-start.2 = (bf16[768,1536]{1,0:T(8,128)(2,1)S(1)}, bf16[768,1536]{1,0:T(8,128)(2,1)}, u32[]{:S(2)}) copy-start(bf16[768,1536]{1,0:T(8,128)(2,1)} %param.13) | copy-start | bytes 7077892
Sparse Core Ops, SparseCore 0:
  29.5 22.1 all-reduce.3
  54.6 35.3 all-reduce.5
  108.3 27.9 reduce-scatter.2
  138.4 20.5 reduce-scatter.4
  176.0 17.9 all-gather.8
  212.2 39.7 all-gather.6
  262.5 19.9 all-reduce.7
